TPU v7x, 32 devices: a whole 2x2x4 slice. The times are simulated.
32 devices in a mesh: space: 8 (over z, x), kern: 4 (over y, core).
Axes of the slice: x: 2, y: 2, z: 4, core: 2. Of those that a mesh axis runs over, the one named last changes fastest.
Arguments:
- mask: bfloat16 [4096, 4096], P('space'), may hold values from -1 to 1
- kernels: float32 [2, 16, 512, 512], P(None, 'kern', 'space'), may hold values from -4 to 4
- target: int32 [1024, 1024], P('space'), may hold values 0 or 1
Outputs:
- gradient: float32 [4096, 4096], P('space')
- resist: float32 [1024, 1024], P('space')
All inputs are finite; a program needn't handle non-finite values. No bound on the sum of `target` on one device may be relied on, other than what follows from the above.
Results may differ from a plain program's by a relative error of at most 0.0003.
Values sent between devices are 32-bit elements; how exact they have to be, the bound alone decides.
A program may use at most 64 MiB of HBM per device.

v0:
```python
import jax
import jax.numpy as jnp
from jax import lax
from jax.sharding import PartitionSpec as P

N = 4096
B = 512
G = 1024
steepness = 8.0
threshold = 1.5
highest = lax.Precision.HIGHEST
block_limit = 1024


def phases(left, right, modulus):
    product = left[:, None] * right[None, :] % modulus
    return product.astype(jnp.float32) * (2.0 * jnp.pi / modulus)


def column_table(pixels, frequency, length):
    angle = phases(pixels, frequency, length)
    return jnp.concatenate([jnp.cos(angle), -jnp.sin(angle)], axis=1)


def row_table(pixels, frequency, length):
    angle = phases(pixels, frequency, length)
    return jnp.concatenate([jnp.cos(angle), -jnp.sin(angle)], axis=1) / length


def grid_table(frequency, points):
    angle = phases(frequency, jnp.arange(points, dtype=jnp.int32), points)
    return jnp.concatenate([jnp.cos(angle), jnp.sin(angle)], axis=1)


def forward_columns(mask, frequency):
    rows = mask.shape[0]
    span = min(block_limit, N)
    count = frequency.shape[0]

    def step(index, running):
        start = index * span
        table = column_table(start + jnp.arange(span, dtype=jnp.int32), frequency, N)
        piece = lax.dynamic_slice_in_dim(mask, start, span, 1).astype(jnp.float32)
        return running + lax.dot_general(table, piece, (((0,), (1,)), ((), ())), precision=highest)

    running = lax.fori_loop(0, N // span, step, jnp.zeros((2 * count, rows), jnp.float32))
    return running.reshape(2, count, rows)


def forward_rows(arrived):
    count = arrived.shape[1]
    flat = arrived.reshape(2 * count, N)
    frequency = jnp.arange(B, dtype=jnp.int32) - B // 2
    span = min(block_limit, N)

    def step(index, running):
        start = index * span
        table = row_table(start + jnp.arange(span, dtype=jnp.int32), frequency, N)
        piece = lax.dynamic_slice_in_dim(flat, start, span, 1)
        return running + jnp.dot(piece, table, precision=highest)

    running = lax.fori_loop(0, N // span, step, jnp.zeros((2 * count, 2 * B), jnp.float32))
    real_part = running[:count, :B] - running[count:, B:]
    imag_part = running[:count, B:] + running[count:, :B]
    return jnp.stack([real_part, imag_part])


def adjoint_rows(sum_re, sum_im):
    count = sum_re.shape[0]
    stacked = jnp.concatenate(
        [jnp.concatenate([sum_re, sum_im], axis=1), jnp.concatenate([sum_im, -sum_re], axis=1)],
        axis=0,
    )
    frequency = jnp.arange(B, dtype=jnp.int32) - B // 2
    span = min(block_limit, N)

    def step(index, output):
        start = index * span
        table = row_table(start + jnp.arange(span, dtype=jnp.int32), frequency, N)
        piece = lax.dot_general(stacked, table, (((1,), (1,)), ((), ())), precision=highest)
        return lax.dynamic_update_slice_in_dim(output, piece, start, 1)

    output = lax.fori_loop(0, N // span, step, jnp.zeros((2 * count, N), jnp.float32))
    return output.reshape(2, count, N)


def add_columns(total, spectrum, frequency):
    span = min(block_limit, N)

    def step(index, running):
        start = index * span
        table = column_table(start + jnp.arange(span, dtype=jnp.int32), frequency, N)
        piece = lax.dot_general(spectrum, table, (((0,), (1,)), ((), ())), precision=highest)
        current = lax.dynamic_slice_in_dim(running, start, span, 1)
        return lax.dynamic_update_slice_in_dim(running, current + piece, start, 1)

    return lax.fori_loop(0, N // span, step, total)


def local(mask, kernels, target):
    rows = mask.shape[0]
    kern_count = lax.axis_size("kern")
    space_count = lax.axis_size("space")
    group = lax.axis_index("kern")
    per_space = B // space_count
    per_group = per_space // kern_count
    frequency = jnp.arange(B, dtype=jnp.int32) - B // 2
    subset = (
        per_space * jnp.arange(space_count, dtype=jnp.int32)[:, None]
        + per_group * group
        + jnp.arange(per_group, dtype=jnp.int32)[None, :]
    )
    columns = forward_columns(mask, subset.reshape(-1) - B // 2)
    arrived = lax.all_to_all(columns, "space", split_axis=1, concat_axis=2, tiled=True)
    spectrum = lax.all_gather(forward_rows(arrived), "kern", axis=1, tiled=True)
    kern_swap = jnp.swapaxes(kernels, 1, 2)
    kernel_count = kern_swap.shape[2]
    spec_re = spectrum[0][:, None, :]
    spec_im = spectrum[1][:, None, :]
    prod_re = kern_swap[0] * spec_re - kern_swap[1] * spec_im
    prod_im = kern_swap[0] * spec_im + kern_swap[1] * spec_re
    grid = grid_table(frequency, G)
    lifted = jnp.dot(
        jnp.stack([prod_re, prod_im]).reshape(2 * per_space * kernel_count, B),
        grid,
        precision=highest,
    )
    lifted = lifted.reshape(2, per_space, kernel_count, 2 * G)
    coarse_re = lifted[0, :, :, :G] - lifted[1, :, :, G:]
    coarse_im = lifted[0, :, :, G:] + lifted[1, :, :, :G]
    coarse = jnp.stack([coarse_re, coarse_im], axis=1)
    gathered = lax.all_to_all(coarse, "space", split_axis=3, concat_axis=0, tiled=True)
    grid_rows = gathered.shape[3]
    image = lax.dot_general(
        gathered.reshape(B, 2 * kernel_count * grid_rows),
        grid,
        (((0,), (0,)), ((), ())),
        precision=highest,
    )
    image = image.reshape(2, kernel_count, grid_rows, 2 * G)
    field_re = image[0, :, :, :G] - image[1, :, :, G:]
    field_im = image[0, :, :, G:] + image[1, :, :, :G]
    partial_light = jnp.sum(field_re * field_re + field_im * field_im, axis=0) / (B * B)
    intensity = lax.psum(partial_light, "kern")
    resist = jax.nn.sigmoid(steepness * (intensity - threshold))
    slope = 2.0 * (resist - target.astype(jnp.float32)) * steepness * resist * (1.0 - resist)
    scale = 2.0 * slope / (B * B)
    grad_re = scale * field_re
    grad_im = scale * field_im
    mixed = jnp.stack(
        [
            jnp.concatenate([grad_re, grad_im], axis=-1),
            jnp.concatenate([grad_im, -grad_re], axis=-1),
        ]
    )
    mixed = mixed.reshape(2 * kernel_count * grid_rows, 2 * G)
    backward = lax.dot_general(grid, mixed, (((1,), (1,)), ((), ())), precision=highest)
    backward = backward.reshape(B, 2, kernel_count, grid_rows)
    returned = lax.all_to_all(backward, "space", split_axis=0, concat_axis=3, tiled=True)
    back_re = returned[:, 0]
    back_im = returned[:, 1]
    mixed_two = jnp.stack(
        [
            jnp.concatenate([back_re, back_im], axis=-1),
            jnp.concatenate([back_im, -back_re], axis=-1),
        ]
    )
    mixed_two = mixed_two.reshape(2 * per_space * kernel_count, 2 * G)
    spectral = lax.dot_general(mixed_two, grid, (((1,), (1,)), ((), ())), precision=highest)
    spectral = spectral.reshape(2, per_space, kernel_count, B)
    sum_re = jnp.sum(kern_swap[0] * spectral[0] + kern_swap[1] * spectral[1], axis=1)
    sum_im = jnp.sum(kern_swap[0] * spectral[1] - kern_swap[1] * spectral[0], axis=1)
    empty = jnp.zeros((rows, N), jnp.float32)
    shares = (
        lax.psum_scatter(sum_re, "kern", scatter_dimension=0, tiled=True),
        lax.psum_scatter(sum_im, "kern", scatter_dimension=0, tiled=True),
    )
    delta = adjoint_rows(shares[0], shares[1])
    landed = lax.all_to_all(delta, "space", split_axis=2, concat_axis=1, tiled=True)
    ordering = (
        per_group * jnp.arange(kern_count, dtype=jnp.int32)[:, None, None]
        + per_space * jnp.arange(space_count, dtype=jnp.int32)[None, :, None]
        + jnp.arange(per_group, dtype=jnp.int32)[None, None, :]
    )
    ordered_freq = ordering.reshape(-1) - B // 2
    piece = lax.all_gather(landed, "kern", axis=1, tiled=True)
    width = piece.shape[1]
    gradient = add_columns(empty, piece.reshape(2 * width, rows), ordered_freq)
    return (gradient, resist)


def solution(mesh):
    in_specs = (P("space", None), P(None, "kern", "space", None), P("space", None))
    out_specs = (P("space", None), P("space", None))
    return jax.shard_map(local, mesh=mesh, in_specs=in_specs, out_specs=out_specs, check_vma=False)
```

profile of v0, /device:TPU:0, one launch (start us, length us, event | category | flops | bytes accessed | tf_op | source)
XLA Modules:
  0.0 641.8 jit_solution(11022036640361063977)
XLA Ops:
  7.2 22.0 %while.66 = (s32[]{:T(128)}, f32[256,512]{1,0:T(8,128)S(1)}, bf16[512,4096]{1,0:T(8,128)(2,1)}, s32[8]{0:T(128)S(1)}, s32[]{:T(128)}, /*index=5*/s32[]{:T(128)}, s32[]{:T(128)}, s32[]{:T(128)}) while((s32[]{:T(128)}, f32[256,512]{1,0:T(8,128)S(1)}, bf16[512,4096]{1,0:T(8,128)(2,1)}, s32[8]{0:T(128)S(1)}, s32[]{:T(128)}, ...), condition=%wide.region_1.2_spmd.clone, body=%wide.region_0.1_spmd.clone.sunk | while | flops 1613104384 | bytes 4204733 | solution.py:46
  37.7 9.6 %fusion.78 = (f32[512,1024]{1,0:T(8,128)S(1)}, f32[512,1024]{1,0:T(8,128)}) fusion(s32[512]{0:T(512)S(1)} %iota_add_fusion.6), kind=kLoop, calls=%fused_computation.130 | loop fusion | flops 7340032 | bytes 4196352 | tf_op jit(solution)/shard_map/cos | solution.py:32
  53.6 47.6 %while.67 = (s32[]{:T(128)}, f32[32,1024]{1,0:T(8,128)S(1)}, f32[32,4096]{1,0:T(8,128)}, s32[]{:T(128)}, s32[]{:T(128)}, /*index=5*/s32[]{:T(128)}, s32[]{:T(128)}) while((s32[]{:T(128)}, f32[32,1024]{1,0:T(8,128)S(1)}, f32[32,4096]{1,0:T(8,128)}, s32[]{:T(128)}, s32[]{:T(128)}, /*index=5*/s32[]{:T(128)}, s32[]{:T(128)}) %tuple.199), condition=%wide.region_3.4_spmd.clone, body=%wide.region_2.3_spmd.clone.sunk | while | flops 412681728 | bytes 8794261 | solution.py:62
  53.9 8.3 %fusion.116 = (f32[1024,512]{1,0:T(8,128)S(1)}, f32[1024,512]{1,0:T(8,128)S(1)}) fusion(s32[512]{0:T(512)S(1)} %iota_add_fusion.17, s32[1024]{0:T(1024)S(1)} %iota_add_fusion.18), kind=kLoop, calls=%fused_computation.79.clone.1 | loop fusion | flops 7864320 | bytes 4200448 | tf_op jit(solution)/shard_map/while/body/eval_jaxpr/cos | solution.py:27
  65.7 8.3 %fusion.116 = (f32[1024,512]{1,0:T(8,128)S(1)}, f32[1024,512]{1,0:T(8,128)S(1)}) fusion(s32[512]{0:T(512)S(1)} %iota_add_fusion.17, s32[1024]{0:T(1024)S(1)} %iota_add_fusion.18), kind=kLoop, calls=%fused_computation.79.clone.1 | loop fusion | flops 7864320 | bytes 4200448 | tf_op jit(solution)/shard_map/while/body/eval_jaxpr/cos | solution.py:27
  77.6 8.3 %fusion.116 = (f32[1024,512]{1,0:T(8,128)S(1)}, f32[1024,512]{1,0:T(8,128)S(1)}) fusion(s32[512]{0:T(512)S(1)} %iota_add_fusion.17, s32[1024]{0:T(1024)S(1)} %iota_add_fusion.18), kind=kLoop, calls=%fused_computation.79.clone.1 | loop fusion | flops 7864320 | bytes 4200448 | tf_op jit(solution)/shard_map/while/body/eval_jaxpr/cos | solution.py:27
  89.4 8.3 %fusion.116 = (f32[1024,512]{1,0:T(8,128)S(1)}, f32[1024,512]{1,0:T(8,128)S(1)}) fusion(s32[512]{0:T(512)S(1)} %iota_add_fusion.17, s32[1024]{0:T(1024)S(1)} %iota_add_fusion.18), kind=kLoop, calls=%fused_computation.79.clone.1 | loop fusion | flops 7864320 | bytes 4200448 | tf_op jit(solution)/shard_map/while/body/eval_jaxpr/cos | solution.py:27
  129.0 53.8 %all_to_all.66 = f32[8,1,65536]{2,1,0:T(1,128)} all-to-all(f32[8,1,65536]{2,1,0:T(1,128)} %reshape.172), channel_id=1, replica_groups=mesh['space'=8,'kern'=4] {'space'}, dimensions={0} | all-to-all | bytes 4194304 | tf_op jit(solution)/shard_map/all_to_all | solution.py:132
  183.3 8.5 %reduce = f32[8,65536]{1,0:T(8,128)} reduce(f32[8,1,65536]{2,1,0:T(1,128)} %all_to_all.66, f32[]{:T(128)} %broadcast.375), dimensions={1}, to_apply=%all_to_all.51.reduce_sub_computation | reduce | bytes 4194308 | tf_op jit(solution)/shard_map/all_to_all | solution.py:132
  209.2 16.7 %fusion.59 = f32[2,4,128,2048]{3,2,1,0:T(8,128)S(1)} fusion(f32[2,4,128,512]{3,2,1,0:T(8,128)} %bitcast.122, f32[512,1024]{1,0:T(8,128)} %get-tuple-element.573, f32[512,1024]{1,0:T(8,128)S(1)} %get-tuple-element.572), kind=kOutput, calls=%fused_computation.95 | convolution fusion | flops 12885950464 | bytes 14680064 | tf_op jit(solution)/shard_map/dot_general | solution.py:134
  230.2 32.4 %all-reduce.2.cloned.1.call-done = f32[128,1024]{1,0:T(8,128)} async-done(((f32[128,1024]{1,0:T(8,128)}), f32[128,1024]{1,0:T(8,128)}) %all-reduce.2.cloned.1.call-update) | async-done | bytes 524304 | tf_op jit(solution)/shard_map/psum | solution.py:144
  273.3 15.5 %fusion.54 = f32[512,2,4,128]{3,0,2,1:T(8,128)S(1)} fusion(f32[1,4,128,2048]{3,2,1,0:T(8,128)} %get-tuple-element.561, f32[1,4,128,2048]{3,2,1,0:T(8,128)} %get-tuple-element.560, f32[512,1024]{1,0:T(8,128)S(1)} %copy-done.3, f32[512,1024]{1,0:T(8,128)S(1)} %get-tuple-element.572), kind=kOutput, calls=%fused_computation.86 | convolution fusion | flops 12888047616 | bytes 14680064 | tf_op jit(solution)/shard_map/dot_general | solution.py:157
  290.1 53.1 %all_to_all.67 = f32[512,2,4,128]{3,2,1,0:T(4,128)S(1)} all-to-all(f32[512,2,4,128]{3,2,1,0:T(4,128)S(1)} %copy.63), channel_id=1, replica_groups=mesh['space'=8,'kern'=4] {'space'}, dimensions={0} | all-to-all | bytes 4194304 | tf_op jit(solution)/shard_map/all_to_all | solution.py:159
  361.6 8.9 %fusion.71 = f32[512,512]{1,0:T(8,128)S(1)} fusion(f32[512,2048]{1,0:T(8,128)} %reshape.168, f32[512,1024]{1,0:T(8,128)} %get-tuple-element.573, f32[512,1024]{1,0:T(8,128)S(1)} %get-tuple-element.572), kind=kOutput, calls=%fused_computation.117 | convolution fusion | flops 6443499520 | bytes 9437184 | tf_op jit(solution)/shard_map/dot_general | solution.py:169
  372.8 17.0 %reduce-scatter.3.cloned.1.call-done = f32[16,512]{1,0:T(8,128)} async-done(((f32[64,512]{1,0:T(8,128)}), f32[16,512]{1,0:T(8,128)}) %reduce-scatter.3.cloned.1.call-update) | async-done | bytes 32784 | tf_op jit(solution)/shard_map/reduce_scatter | solution.py:175
  390.5 21.9 %reduce-scatter.5.cloned.1.call-done = f32[16,512]{1,0:T(8,128)} async-done(((f32[64,512]{1,0:T(8,128)}), f32[16,512]{1,0:T(8,128)}) %reduce-scatter.5.cloned.1.call-update) | async-done | bytes 32784 | tf_op jit(solution)/shard_map/reduce_scatter | solution.py:176
  413.3 49.2 %while.64 = (s32[]{:T(128)}, f32[32,4096]{1,0:T(8,128)S(1)}, f32[32,1024]{1,0:T(8,128)S(1)}, s32[]{:T(128)}, s32[]{:T(128)}, /*index=5*/s32[]{:T(128)}, s32[]{:T(128)}) while((s32[]{:T(128)}, f32[32,4096]{1,0:T(8,128)S(1)}, f32[32,1024]{1,0:T(8,128)S(1)}, s32[]{:T(128)}, s32[]{:T(128)}, /*index=5*/s32[]{:T(128)}, ...), condition=%wide.region_11.12_spmd.clone, body=%wide.region_10.11_spmd.clone.sunk | while | flops 412616192 | bytes 8663171 | solution.py:83
  413.5 8.3 %fusion.107 = (f32[1024,512]{1,0:T(8,128)S(1)}, f32[1024,512]{1,0:T(8,128)S(1)}) fusion(s32[512]{0:T(512)S(1)} %iota_add_fusion.13, s32[1024]{0:T(1024)S(1)} %iota_add_fusion.14), kind=kLoop, calls=%fused_computation.20.clone.1 | loop fusion | flops 7864320 | bytes 4200448 | tf_op jit(solution)/shard_map/while/body/eval_jaxpr/cos | solution.py:27
  425.8 8.3 %fusion.107 = (f32[1024,512]{1,0:T(8,128)S(1)}, f32[1024,512]{1,0:T(8,128)S(1)}) fusion(s32[512]{0:T(512)S(1)} %iota_add_fusion.13, s32[1024]{0:T(1024)S(1)} %iota_add_fusion.14), kind=kLoop, calls=%fused_computation.20.clone.1 | loop fusion | flops 7864320 | bytes 4200448 | tf_op jit(solution)/shard_map/while/body/eval_jaxpr/cos | solution.py:27
  438.0 8.3 %fusion.107 = (f32[1024,512]{1,0:T(8,128)S(1)}, f32[1024,512]{1,0:T(8,128)S(1)}) fusion(s32[512]{0:T(512)S(1)} %iota_add_fusion.13, s32[1024]{0:T(1024)S(1)} %iota_add_fusion.14), kind=kLoop, calls=%fused_computation.20.clone.1 | loop fusion | flops 7864320 | bytes 4200448 | tf_op jit(solution)/shard_map/while/body/eval_jaxpr/cos | solution.py:27
  450.3 8.3 %fusion.107 = (f32[1024,512]{1,0:T(8,128)S(1)}, f32[1024,512]{1,0:T(8,128)S(1)}) fusion(s32[512]{0:T(512)S(1)} %iota_add_fusion.13, s32[1024]{0:T(1024)S(1)} %iota_add_fusion.14), kind=kLoop, calls=%fused_computation.20.clone.1 | loop fusion | flops 7864320 | bytes 4200448 | tf_op jit(solution)/shard_map/while/body/eval_jaxpr/cos | solution.py:27
  474.2 19.3 %all_to_all.68 = f32[8,1,16384]{2,1,0:T(1,128)S(1)} all-to-all(f32[8,1,16384]{2,1,0:T(1,128)S(1)} %reshape.174), channel_id=1, replica_groups=mesh['space'=8,'kern'=4] {'space'}, dimensions={0} | all-to-all | bytes 1048576 | tf_op jit(solution)/shard_map/all_to_all | solution.py:179
  509.4 20.8 %all-gather.2.cloned.1.call-done = f32[2,512,512]{2,1,0:T(8,128)} async-done(((f32[2,128,512]{2,1,0:T(8,128)}), f32[2,512,512]{2,1,0:T(8,128)}) %all-gather.2.cloned.1.call-update) | async-done | bytes 2097168 | tf_op jit(solution)/shard_map/all_gather | solution.py:186
  534.6 100.2 %while.65 = (s32[]{:T(128)}, f32[512,4096]{1,0:T(8,128)}, f32[1024,512]{1,0:T(8,128)}, s32[4,8]{1,0:T(4,128)S(1)}, s32[]{:T(128)}, /*index=5*/s32[]{:T(128)}, s32[]{:T(128)}, s32[]{:T(128)}) while((s32[]{:T(128)}, f32[512,4096]{1,0:T(8,128)}, f32[1024,512]{1,0:T(8,128)}, s32[4,8]{1,0:T(4,128)S(1)}, s32[]{:T(128)}, ...), condition=%wide.region_13.14_spmd.clone, body=%wide.region_12.13_spmd.clone.sunk | while | flops 6451890176 | bytes 39862572 | solution.py:97
  540.2 8.3 %fusion.111 = (f32[1024,512]{1,0:T(8,128)S(1)}, f32[1024,512]{1,0:T(8,128)S(1)}) fusion(s32[512]{0:T(512)S(1)} %sub.133, s32[1024]{0:T(1024)S(1)} %iota_add_fusion.15), kind=kLoop, calls=%fused_computation.39.clone.1 | loop fusion | flops 7864320 | bytes 4200448 | tf_op jit(solution)/shard_map/while/body/eval_jaxpr/cos | solution.py:22
  548.5 8.0 %bitcast_add_fusion.2 = f32[512,1024]{0,1:T(8,128)} fusion(f32[512,1024]{0,1:T(8,128)S(1)} %copy.92, f32[1024,512]{1,0:T(8,128)S(1)} %copy-done.1, f32[1024,512]{1,0:T(8,128)S(1)} %get-tuple-element.665, f32[1024,512]{1,0:T(8,128)S(1)} %get-tuple-element.666), kind=kOutput, calls=%fused_computation.37.clone.1 | convolution fusion | flops 6444023808 | bytes 10485760 | tf_op jit(solution)/shard_map/while/body/eval_jaxpr/dot_general | solution.py:93
  565.1 8.3 %fusion.111 = (f32[1024,512]{1,0:T(8,128)S(1)}, f32[1024,512]{1,0:T(8,128)S(1)}) fusion(s32[512]{0:T(512)S(1)} %sub.133, s32[1024]{0:T(1024)S(1)} %iota_add_fusion.15), kind=kLoop, calls=%fused_computation.39.clone.1 | loop fusion | flops 7864320 | bytes 4200448 | tf_op jit(solution)/shard_map/while/body/eval_jaxpr/cos | solution.py:22
  573.4 8.0 %bitcast_add_fusion.2 = f32[512,1024]{0,1:T(8,128)} fusion(f32[512,1024]{0,1:T(8,128)S(1)} %copy.92, f32[1024,512]{1,0:T(8,128)S(1)} %copy-done.1, f32[1024,512]{1,0:T(8,128)S(1)} %get-tuple-element.665, f32[1024,512]{1,0:T(8,128)S(1)} %get-tuple-element.666), kind=kOutput, calls=%fused_computation.37.clone.1 | convolution fusion | flops 6444023808 | bytes 10485760 | tf_op jit(solution)/shard_map/while/body/eval_jaxpr/dot_general | solution.py:93
  590.1 8.3 %fusion.111 = (f32[1024,512]{1,0:T(8,128)S(1)}, f32[1024,512]{1,0:T(8,128)S(1)}) fusion(s32[512]{0:T(512)S(1)} %sub.133, s32[1024]{0:T(1024)S(1)} %iota_add_fusion.15), kind=kLoop, calls=%fused_computation.39.clone.1 | loop fusion | flops 7864320 | bytes 4200448 | tf_op jit(solution)/shard_map/while/body/eval_jaxpr/cos | solution.py:22
  598.4 8.0 %bitcast_add_fusion.2 = f32[512,1024]{0,1:T(8,128)} fusion(f32[512,1024]{0,1:T(8,128)S(1)} %copy.92, f32[1024,512]{1,0:T(8,128)S(1)} %copy-done.1, f32[1024,512]{1,0:T(8,128)S(1)} %get-tuple-element.665, f32[1024,512]{1,0:T(8,128)S(1)} %get-tuple-element.666), kind=kOutput, calls=%fused_computation.37.clone.1 | convolution fusion | flops 6444023808 | bytes 10485760 | tf_op jit(solution)/shard_map/while/body/eval_jaxpr/dot_general | solution.py:93
  615.1 8.3 %fusion.111 = (f32[1024,512]{1,0:T(8,128)S(1)}, f32[1024,512]{1,0:T(8,128)S(1)}) fusion(s32[512]{0:T(512)S(1)} %sub.133, s32[1024]{0:T(1024)S(1)} %iota_add_fusion.15), kind=kLoop, calls=%fused_computation.39.clone.1 | loop fusion | flops 7864320 | bytes 4200448 | tf_op jit(solution)/shard_map/while/body/eval_jaxpr/cos | solution.py:22
  623.4 8.0 %bitcast_add_fusion.2 = f32[512,1024]{0,1:T(8,128)} fusion(f32[512,1024]{0,1:T(8,128)S(1)} %copy.92, f32[1024,512]{1,0:T(8,128)S(1)} %copy-done.1, f32[1024,512]{1,0:T(8,128)S(1)} %get-tuple-element.665, f32[1024,512]{1,0:T(8,128)S(1)} %get-tuple-element.666), kind=kOutput, calls=%fused_computation.37.clone.1 | convolution fusion | flops 6444023808 | bytes 10485760 | tf_op jit(solution)/shard_map/while/body/eval_jaxpr/dot_general | solution.py:93
  (153 shorter events, 216.9 us)
Async XLA Ops:
  30.4 21.7 %all-to-all-start = ((f32[2,128,512]{2,0,1:T(2,128)}), f32[2,128,512]{2,0,1:T(2,128)S(1)}, u32[]{:S(2)}, u32[]{:S(2)}) async-start(f32[2,128,512]{2,0,1:T(2,128)} %copy.57), calls=%async_computation | async-start | bytes 1048576 | tf_op jit(solution)/shard_map/all_to_all | solution.py:114
  37.6 225.0 %all-reduce.2.cloned.1.call-start = ((), (), s32[]{:S(2)}) async-start(), calls=%async_computation.6 | async-start | bytes 1048576 | tf_op jit(solution)/shard_map/psum | solution.py:144
  53.6 53.8 %copy-start.5 = (f32[2,4,64,512]{3,2,1,0:T(8,128)S(1)}, f32[2,4,64,512]{3,2,1,0:T(8,128)}, u32[]{:S(2)}) copy-start(f32[2,4,64,512]{3,2,1,0:T(8,128)} %param.12) | copy-start | bytes 3145732
  101.2 6.5 %copy-start.2 = (f32[512,1024]{1,0:T(8,128)S(1)}, f32[512,1024]{1,0:T(8,128)}, u32[]{:S(2)}) copy-start(f32[512,1024]{1,0:T(8,128)} %get-tuple-element.573) | copy-start | bytes 6291460
  225.9 3.4 copy-start
  230.2 159.6 %reduce-scatter.3.cloned.1.call-start = ((), (), s32[]{:S(2)}) async-start(), calls=%async_computation.7 | async-start | bytes 163840 | tf_op jit(solution)/shard_map/reduce_scatter | solution.py:175
  269.3 4.0 copy-start.3
  348.5 1.9 copy-start.4
  372.0 40.5 %reduce-scatter.5.cloned.1.call-start = ((), (), s32[]{:S(2)}) async-start(), calls=%async_computation.8 | async-start | bytes 163840 | tf_op jit(solution)/shard_map/reduce_scatter | solution.py:176
  372.7 157.5 %all-gather.2.cloned.1.call-start = ((), (), s32[]{:S(2)}) async-start(), calls=%async_computation.9 | async-start | bytes 2621440 | tf_op jit(solution)/shard_map/all_gather | solution.py:186
  540.1 8.3 %copy-start.1 = (f32[1024,512]{1,0:T(8,128)S(1)}, f32[1024,512]{1,0:T(8,128)}, u32[]{:S(2)}) copy-start(f32[1024,512]{1,0:T(8,128)} %get-tuple-element.762) | copy-start | bytes 6291460 | tf_op jit(solution)/shard_map/while
  565.1 8.3 %copy-start.1 = (f32[1024,512]{1,0:T(8,128)S(1)}, f32[1024,512]{1,0:T(8,128)}, u32[]{:S(2)}) copy-start(f32[1024,512]{1,0:T(8,128)} %get-tuple-element.762) | copy-start | bytes 6291460 | tf_op jit(solution)/shard_map/while
  590.1 8.3 %copy-start.1 = (f32[1024,512]{1,0:T(8,128)S(1)}, f32[1024,512]{1,0:T(8,128)}, u32[]{:S(2)}) copy-start(f32[1024,512]{1,0:T(8,128)} %get-tuple-element.762) | copy-start | bytes 6291460 | tf_op jit(solution)/shard_map/while
  615.1 8.3 %copy-start.1 = (f32[1024,512]{1,0:T(8,128)S(1)}, f32[1024,512]{1,0:T(8,128)}, u32[]{:S(2)}) copy-start(f32[1024,512]{1,0:T(8,128)} %get-tuple-element.762) | copy-start | bytes 6291460 | tf_op jit(solution)/shard_map/while
Sparse Core Ops, SparseCore 0:
  230.3 32.2 all-reduce.1
  372.1 17.5 reduce-scatter.2
  392.9 19.5 reduce-scatter.4
  509.4 20.7 all-gather.1
where the time goes:
time: 649 us; the launch traced here: 642 us
  other arithmetic  149 us (23%)
  blocking collectives  132 us (20%)
  matrix products  122 us (19%)
  local copies, waits for them, and re-layouts  118 us (18%)
  waiting for transfers between devices  97.6 us (15%)
  between operations  14.5 us (2%)
  starting transfers between devices  7.41 us (1%)
    cos x8, other arithmetic, row_table(): return jnp.concatenate([jnp.cos(angle), -jnp.sin(angle)], axis=1) / length  66.3 us
    all_to_all x1, blocking collectives, local(): lax.all_to_all(coarse, 'space', split_axis=3, concat_axis=0, tiled=True)  53.8 us
    all_to_all x1, blocking collectives, local(): lax.all_to_all(backward, 'space', split_axis=0, concat_axis=3, tiled=True)  53.1 us
    cos x8, other arithmetic, column_table(): return jnp.concatenate([jnp.cos(angle), -jnp.sin(angle)], axis=1)  41.7 us
    unnamed x15, local copies, waits for them, and re-layouts  33.1 us
    psum x1, waiting for transfers between devices, local(): intensity = lax.psum(partial_light, 'kern')  32.4 us
    dot_general x4, matrix products, step(): lax.dot_general(spectrum, table, (((0,), (1,)), ((), ())), precision=high...  32.1 us
    reduce_scatter x1, waiting for transfers between devices, local(): lax.psum_scatter(sum_im, 'kern', scatter_dimension=0, tiled=True)  21.9 us
  transfers between devices with their start and end apart: 5, of which 5 were waited for; matrix products, arithmetic and copies ran while one was open for 2% of the time, Pallas kernels for 0%

commit v1 on v0

--- a/solution.py
+++ b/solution.py
@@ -129,7 +129,27 @@
     coarse_re = lifted[0, :, :, :G] - lifted[1, :, :, G:]
     coarse_im = lifted[0, :, :, G:] + lifted[1, :, :, :G]
     coarse = jnp.stack([coarse_re, coarse_im], axis=1)
-    gathered = lax.all_to_all(coarse, "space", split_axis=3, concat_axis=0, tiled=True)
+
+    def state_page(point):
+        lower, outer = (lax.axis_size("space"), lax.axis_index("space"))
+        current_arr = point.shape[3] // lower
+        newest = list(point.shape)
+        newest[3] = current_arr
+        finding = newest[0]
+        newest[0] = finding * lower
+        r2 = jnp.zeros(newest, point.dtype)
+        for dev in range(lower):
+            found_now = lax.dynamic_slice_in_dim(
+                point, (outer ^ dev) * current_arr, current_arr, axis=3
+            )
+            if dev:
+                found_now = lax.ppermute(
+                    found_now, "space", list(map(lambda at: (at, at ^ dev), range(lower)))
+                )
+            r2 = lax.dynamic_update_slice_in_dim(r2, found_now, (outer ^ dev) * finding, axis=0)
+        return r2
+
+    gathered = state_page(coarse)
     grid_rows = gathered.shape[3]
     image = lax.dot_general(
         gathered.reshape(B, 2 * kernel_count * grid_rows),

time: 649 us -> 618 us (0.952)
  blocking collectives: 132 us -> 78.7 us
  starting transfers between devices: 7.41 us -> 17.8 us
  waiting for transfers between devices: 97.6 us -> 107 us
  local copies, waits for them, and re-layouts: 118 us -> 127 us
  other arithmetic: 149 us -> 141 us
    all_to_all x1 -> x0, blocking collectives: 53.8 us -> none  [local(): lax.all_to_all(coarse, 'space', split_axis=3, concat_axis=0, tiled=True)]
    dynamic_update_slice x0 -> x8, local copies, waits for them, and re-layouts: none -> 29.8 us  [state_page(): lax.dynamic_update_slice_in_dim(r2, found_now, (outer ^ dev) * finding, a...]
    unnamed x15 -> x19, local copies, waits for them, and re-layouts: 33.1 us -> 20.6 us
    ppermute x0 -> x7, starting transfers between devices: none -> 10.4 us  [state_page(): lax.ppermute(found_now, 'space', list(map(lambda at: (at, at ^ dev), rang...]
    ppermute x0 -> x7, waiting for transfers between devices: none -> 9 us  [state_page(): lax.ppermute(found_now, 'space', list(map(lambda at: (at, at ^ dev), rang...]
    all_to_all x1 -> x0, other arithmetic: 8.52 us -> none  [local(): lax.all_to_all(coarse, 'space', split_axis=3, concat_axis=0, tiled=True)]
  transfers between devices with their start and end apart: 5 -> 12, of which waited for: 5 -> 6; matrix products, arithmetic and copies ran while one was open for 2% -> 8% of each run, Pallas kernels for 0% -> 0%
where the time goes in v1:
time: 618 us; the launch traced here: 611 us
  other arithmetic  141 us (23%)
  local copies, waits for them, and re-layouts  127 us (21%)
  matrix products  122 us (20%)
  waiting for transfers between devices  107 us (17%)
  blocking collectives  78.7 us (13%)
  starting transfers between devices  17.8 us (3%)
  between operations  14.7 us (2%)
    cos x8, other arithmetic, row_table(): return jnp.concatenate([jnp.cos(angle), -jnp.sin(angle)], axis=1) / length  66.3 us
    all_to_all x1, blocking collectives, local(): lax.all_to_all(backward, 'space', split_axis=0, concat_axis=3, tiled=True)  53.1 us
    cos x8, other arithmetic, column_table(): return jnp.concatenate([jnp.cos(angle), -jnp.sin(angle)], axis=1)  41.7 us
    psum x1, waiting for transfers between devices, local(): intensity = lax.psum(partial_light, 'kern')  33.1 us
    dot_general x4, matrix products, step(): lax.dot_general(spectrum, table, (((0,), (1,)), ((), ())), precision=high...  32 us
    dynamic_update_slice x8, local copies, waits for them, and re-layouts, state_page(): lax.dynamic_update_slice_in_dim(r2, found_now, (outer ^ dev) * finding, a...  29.8 us
    reduce_scatter x1, waiting for transfers between devices, local(): lax.psum_scatter(sum_im, 'kern', scatter_dimension=0, tiled=True)  22 us
    all_gather x1, waiting for transfers between devices, local(): piece = lax.all_gather(landed, 'kern', axis=1, tiled=True)  20.8 us
  transfers between devices with their start and end apart: 12, of which 6 were waited for; matrix products, arithmetic and copies ran while one was open for 8% of the time, Pallas kernels for 0%

profile of v1, /device:TPU:0, one launch (start us, length us, event | category | flops | bytes accessed | tf_op | source)
XLA Modules:
  0.0 610.6 jit_solution(11609482439682798718)
XLA Ops:
  7.2 22.0 %while.66 = (s32[]{:T(128)}, f32[256,512]{1,0:T(8,128)S(1)}, bf16[512,4096]{1,0:T(8,128)(2,1)}, s32[8]{0:T(128)S(1)}, s32[]{:T(128)}, /*index=5*/s32[]{:T(128)}, s32[]{:T(128)}, s32[]{:T(128)}) while((s32[]{:T(128)}, f32[256,512]{1,0:T(8,128)S(1)}, bf16[512,4096]{1,0:T(8,128)(2,1)}, s32[8]{0:T(128)S(1)}, s32[]{:T(128)}, ...), condition=%wide.region_1.2_spmd.clone, body=%wide.region_0.1_spmd.clone.sunk | while | flops 1613104384 | bytes 4204733 | solution.py:46
  37.7 9.6 %fusion.79 = (f32[512,1024]{1,0:T(8,128)S(1)}, f32[512,1024]{1,0:T(8,128)}) fusion(s32[512]{0:T(512)S(1)} %iota_add_fusion.6), kind=kLoop, calls=%fused_computation.146 | loop fusion | flops 7340032 | bytes 4196352 | tf_op jit(solution)/shard_map/cos | solution.py:32
  53.6 47.6 %while.67 = (s32[]{:T(128)}, f32[32,1024]{1,0:T(8,128)S(1)}, f32[32,4096]{1,0:T(8,128)}, s32[]{:T(128)}, s32[]{:T(128)}, /*index=5*/s32[]{:T(128)}, s32[]{:T(128)}) while((s32[]{:T(128)}, f32[32,1024]{1,0:T(8,128)S(1)}, f32[32,4096]{1,0:T(8,128)}, s32[]{:T(128)}, s32[]{:T(128)}, /*index=5*/s32[]{:T(128)}, s32[]{:T(128)}) %tuple.205), condition=%wide.region_3.4_spmd.clone, body=%wide.region_2.3_spmd.clone.sunk | while | flops 412681728 | bytes 8794261 | solution.py:62
  53.9 8.3 %fusion.124 = (f32[1024,512]{1,0:T(8,128)S(1)}, f32[1024,512]{1,0:T(8,128)S(1)}) fusion(s32[512]{0:T(512)S(1)} %iota_add_fusion.17, s32[1024]{0:T(1024)S(1)} %iota_add_fusion.18), kind=kLoop, calls=%fused_computation.79.clone.1 | loop fusion | flops 7864320 | bytes 4200448 | tf_op jit(solution)/shard_map/while/body/eval_jaxpr/cos | solution.py:27
  65.7 8.3 %fusion.124 = (f32[1024,512]{1,0:T(8,128)S(1)}, f32[1024,512]{1,0:T(8,128)S(1)}) fusion(s32[512]{0:T(512)S(1)} %iota_add_fusion.17, s32[1024]{0:T(1024)S(1)} %iota_add_fusion.18), kind=kLoop, calls=%fused_computation.79.clone.1 | loop fusion | flops 7864320 | bytes 4200448 | tf_op jit(solution)/shard_map/while/body/eval_jaxpr/cos | solution.py:27
  77.6 8.3 %fusion.124 = (f32[1024,512]{1,0:T(8,128)S(1)}, f32[1024,512]{1,0:T(8,128)S(1)}) fusion(s32[512]{0:T(512)S(1)} %iota_add_fusion.17, s32[1024]{0:T(1024)S(1)} %iota_add_fusion.18), kind=kLoop, calls=%fused_computation.79.clone.1 | loop fusion | flops 7864320 | bytes 4200448 | tf_op jit(solution)/shard_map/while/body/eval_jaxpr/cos | solution.py:27
  89.4 8.3 %fusion.124 = (f32[1024,512]{1,0:T(8,128)S(1)}, f32[1024,512]{1,0:T(8,128)S(1)}) fusion(s32[512]{0:T(512)S(1)} %iota_add_fusion.17, s32[1024]{0:T(1024)S(1)} %iota_add_fusion.18), kind=kLoop, calls=%fused_computation.79.clone.1 | loop fusion | flops 7864320 | bytes 4200448 | tf_op jit(solution)/shard_map/while/body/eval_jaxpr/cos | solution.py:27
  127.8 9.0 %collective-permute-done.1 = f32[64,2,4,128]{3,0,2,1:T(8,128)} collective-permute-done((f32[64,2,4,128]{3,0,2,1:T(8,128)}, f32[64,2,4,128]{3,0,2,1:T(8,128)}, u32[]{:S(2)}, u32[]{:S(2)}) %collective-permute-start.1) | collective-permute-done | bytes 262176 | tf_op jit(solution)/shard_map/ppermute | solution.py:146
  176.3 16.7 %fusion.59 = f32[2,4,128,2048]{3,2,1,0:T(8,128)S(1)} fusion(f32[512,2,4,128]{0,3,2,1:T(8,128)} %dynamic_update_slice.51, f32[512,1024]{1,0:T(8,128)} %get-tuple-element.581, f32[512,1024]{1,0:T(8,128)S(1)} %get-tuple-element.580), kind=kOutput, calls=%fused_computation.111 | convolution fusion | flops 12885950464 | bytes 14680064 | tf_op jit(solution)/shard_map/dot_general | solution.py:154
  197.3 33.1 %all-reduce.2.cloned.1.call-done = f32[128,1024]{1,0:T(8,128)} async-done(((f32[128,1024]{1,0:T(8,128)}), f32[128,1024]{1,0:T(8,128)}) %all-reduce.2.cloned.1.call-update) | async-done | bytes 524304 | tf_op jit(solution)/shard_map/psum | solution.py:164
  240.9 15.5 %fusion.54 = f32[512,2,4,128]{3,0,2,1:T(8,128)S(1)} fusion(f32[1,4,128,2048]{3,2,1,0:T(8,128)} %get-tuple-element.561, f32[1,4,128,2048]{3,2,1,0:T(8,128)} %get-tuple-element.560, f32[512,1024]{1,0:T(8,128)S(1)} %copy-done.3, f32[512,1024]{1,0:T(8,128)S(1)} %get-tuple-element.580), kind=kOutput, calls=%fused_computation.86 | convolution fusion | flops 12888047616 | bytes 14680064 | tf_op jit(solution)/shard_map/dot_general | solution.py:177
  257.7 53.1 %all_to_all.51 = f32[512,2,4,128]{3,2,1,0:T(4,128)S(1)} all-to-all(f32[512,2,4,128]{3,2,1,0:T(4,128)S(1)} %copy.90), channel_id=1, replica_groups=mesh['space'=8,'kern'=4] {'space'}, dimensions={0} | all-to-all | bytes 4194304 | tf_op jit(solution)/shard_map/all_to_all | solution.py:179
  329.1 8.9 %fusion.72 = f32[512,512]{1,0:T(8,128)S(1)} fusion(f32[512,2048]{1,0:T(8,128)} %reshape.167, f32[512,1024]{1,0:T(8,128)} %get-tuple-element.581, f32[512,1024]{1,0:T(8,128)S(1)} %get-tuple-element.580), kind=kOutput, calls=%fused_computation.133 | convolution fusion | flops 6443499520 | bytes 9437184 | tf_op jit(solution)/shard_map/dot_general | solution.py:189
  341.2 17.0 %reduce-scatter.3.cloned.1.call-done = f32[16,512]{1,0:T(8,128)} async-done(((f32[64,512]{1,0:T(8,128)}), f32[16,512]{1,0:T(8,128)}) %reduce-scatter.3.cloned.1.call-update) | async-done | bytes 32784 | tf_op jit(solution)/shard_map/reduce_scatter | solution.py:195
  358.9 22.0 %reduce-scatter.5.cloned.1.call-done = f32[16,512]{1,0:T(8,128)} async-done(((f32[64,512]{1,0:T(8,128)}), f32[16,512]{1,0:T(8,128)}) %reduce-scatter.5.cloned.1.call-update) | async-done | bytes 32784 | tf_op jit(solution)/shard_map/reduce_scatter | solution.py:196
  381.8 49.2 %while.64 = (s32[]{:T(128)}, f32[32,4096]{1,0:T(8,128)S(1)}, f32[32,1024]{1,0:T(8,128)S(1)}, s32[]{:T(128)}, s32[]{:T(128)}, /*index=5*/s32[]{:T(128)}, s32[]{:T(128)}) while((s32[]{:T(128)}, f32[32,4096]{1,0:T(8,128)S(1)}, f32[32,1024]{1,0:T(8,128)S(1)}, s32[]{:T(128)}, s32[]{:T(128)}, /*index=5*/s32[]{:T(128)}, ...), condition=%wide.region_11.12_spmd.clone, body=%wide.region_10.11_spmd.clone.sunk | while | flops 412616192 | bytes 8663171 | solution.py:83
  382.0 8.3 %fusion.115 = (f32[1024,512]{1,0:T(8,128)S(1)}, f32[1024,512]{1,0:T(8,128)S(1)}) fusion(s32[512]{0:T(512)S(1)} %iota_add_fusion.13, s32[1024]{0:T(1024)S(1)} %iota_add_fusion.14), kind=kLoop, calls=%fused_computation.20.clone.1 | loop fusion | flops 7864320 | bytes 4200448 | tf_op jit(solution)/shard_map/while/body/eval_jaxpr/cos | solution.py:27
  394.2 8.3 %fusion.115 = (f32[1024,512]{1,0:T(8,128)S(1)}, f32[1024,512]{1,0:T(8,128)S(1)}) fusion(s32[512]{0:T(512)S(1)} %iota_add_fusion.13, s32[1024]{0:T(1024)S(1)} %iota_add_fusion.14), kind=kLoop, calls=%fused_computation.20.clone.1 | loop fusion | flops 7864320 | bytes 4200448 | tf_op jit(solution)/shard_map/while/body/eval_jaxpr/cos | solution.py:27
  406.5 8.3 %fusion.115 = (f32[1024,512]{1,0:T(8,128)S(1)}, f32[1024,512]{1,0:T(8,128)S(1)}) fusion(s32[512]{0:T(512)S(1)} %iota_add_fusion.13, s32[1024]{0:T(1024)S(1)} %iota_add_fusion.14), kind=kLoop, calls=%fused_computation.20.clone.1 | loop fusion | flops 7864320 | bytes 4200448 | tf_op jit(solution)/shard_map/while/body/eval_jaxpr/cos | solution.py:27
  418.7 8.3 %fusion.115 = (f32[1024,512]{1,0:T(8,128)S(1)}, f32[1024,512]{1,0:T(8,128)S(1)}) fusion(s32[512]{0:T(512)S(1)} %iota_add_fusion.13, s32[1024]{0:T(1024)S(1)} %iota_add_fusion.14), kind=kLoop, calls=%fused_computation.20.clone.1 | loop fusion | flops 7864320 | bytes 4200448 | tf_op jit(solution)/shard_map/while/body/eval_jaxpr/cos | solution.py:27
  442.7 19.3 %all_to_all.52 = f32[8,1,16384]{2,1,0:T(1,128)S(1)} all-to-all(f32[8,1,16384]{2,1,0:T(1,128)S(1)} %reshape.171), channel_id=1, replica_groups=mesh['space'=8,'kern'=4] {'space'}, dimensions={0} | all-to-all | bytes 1048576 | tf_op jit(solution)/shard_map/all_to_all | solution.py:199
  464.4 7.6 %reshape.172 = f32[4096,2,16]{2,1,0:T(2,128)} reshape(f32[8,16384]{1,0:T(8,128)S(1)} %reduce) | data formatting | bytes 1048576
  478.4 20.8 %all-gather.2.cloned.1.call-done = f32[2,512,512]{2,1,0:T(8,128)} async-done(((f32[2,128,512]{2,1,0:T(8,128)}), f32[2,512,512]{2,1,0:T(8,128)}) %all-gather.2.cloned.1.call-update) | async-done | bytes 2097168 | tf_op jit(solution)/shard_map/all_gather | solution.py:206
  503.6 100.0 %while.65 = (s32[]{:T(128)}, f32[512,4096]{1,0:T(8,128)}, f32[1024,512]{1,0:T(8,128)}, s32[4,8]{1,0:T(4,128)S(1)}, s32[]{:T(128)}, /*index=5*/s32[]{:T(128)}, s32[]{:T(128)}, s32[]{:T(128)}) while((s32[]{:T(128)}, f32[512,4096]{1,0:T(8,128)}, f32[1024,512]{1,0:T(8,128)}, s32[4,8]{1,0:T(4,128)S(1)}, s32[]{:T(128)}, ...), condition=%wide.region_13.14_spmd.clone, body=%wide.region_12.13_spmd.clone.sunk | while | flops 6451890176 | bytes 39862572 | solution.py:97
  509.1 8.3 %fusion.119 = (f32[1024,512]{1,0:T(8,128)S(1)}, f32[1024,512]{1,0:T(8,128)S(1)}) fusion(s32[512]{0:T(512)S(1)} %sub.133, s32[1024]{0:T(1024)S(1)} %iota_add_fusion.15), kind=kLoop, calls=%fused_computation.39.clone.1 | loop fusion | flops 7864320 | bytes 4200448 | tf_op jit(solution)/shard_map/while/body/eval_jaxpr/cos | solution.py:22
  517.4 8.0 %bitcast_add_fusion.2 = f32[512,1024]{0,1:T(8,128)} fusion(f32[512,1024]{0,1:T(8,128)S(1)} %copy.119, f32[1024,512]{1,0:T(8,128)S(1)} %copy-done.1, f32[1024,512]{1,0:T(8,128)S(1)} %get-tuple-element.673, f32[1024,512]{1,0:T(8,128)S(1)} %get-tuple-element.674), kind=kOutput, calls=%fused_computation.37.clone.1 | convolution fusion | flops 6444023808 | bytes 10485760 | tf_op jit(solution)/shard_map/while/body/eval_jaxpr/dot_general | solution.py:93
  534.0 8.3 %fusion.119 = (f32[1024,512]{1,0:T(8,128)S(1)}, f32[1024,512]{1,0:T(8,128)S(1)}) fusion(s32[512]{0:T(512)S(1)} %sub.133, s32[1024]{0:T(1024)S(1)} %iota_add_fusion.15), kind=kLoop, calls=%fused_computation.39.clone.1 | loop fusion | flops 7864320 | bytes 4200448 | tf_op jit(solution)/shard_map/while/body/eval_jaxpr/cos | solution.py:22
  542.3 8.0 %bitcast_add_fusion.2 = f32[512,1024]{0,1:T(8,128)} fusion(f32[512,1024]{0,1:T(8,128)S(1)} %copy.119, f32[1024,512]{1,0:T(8,128)S(1)} %copy-done.1, f32[1024,512]{1,0:T(8,128)S(1)} %get-tuple-element.673, f32[1024,512]{1,0:T(8,128)S(1)} %get-tuple-element.674), kind=kOutput, calls=%fused_computation.37.clone.1 | convolution fusion | flops 6444023808 | bytes 10485760 | tf_op jit(solution)/shard_map/while/body/eval_jaxpr/dot_general | solution.py:93
  559.0 8.3 %fusion.119 = (f32[1024,512]{1,0:T(8,128)S(1)}, f32[1024,512]{1,0:T(8,128)S(1)}) fusion(s32[512]{0:T(512)S(1)} %sub.133, s32[1024]{0:T(1024)S(1)} %iota_add_fusion.15), kind=kLoop, calls=%fused_computation.39.clone.1 | loop fusion | flops 7864320 | bytes 4200448 | tf_op jit(solution)/shard_map/while/body/eval_jaxpr/cos | solution.py:22
  567.3 8.0 %bitcast_add_fusion.2 = f32[512,1024]{0,1:T(8,128)} fusion(f32[512,1024]{0,1:T(8,128)S(1)} %copy.119, f32[1024,512]{1,0:T(8,128)S(1)} %copy-done.1, f32[1024,512]{1,0:T(8,128)S(1)} %get-tuple-element.673, f32[1024,512]{1,0:T(8,128)S(1)} %get-tuple-element.674), kind=kOutput, calls=%fused_computation.37.clone.1 | convolution fusion | flops 6444023808 | bytes 10485760 | tf_op jit(solution)/shard_map/while/body/eval_jaxpr/dot_general | solution.py:93
  583.9 8.3 %fusion.119 = (f32[1024,512]{1,0:T(8,128)S(1)}, f32[1024,512]{1,0:T(8,128)S(1)}) fusion(s32[512]{0:T(512)S(1)} %sub.133, s32[1024]{0:T(1024)S(1)} %iota_add_fusion.15), kind=kLoop, calls=%fused_computation.39.clone.1 | loop fusion | flops 7864320 | bytes 4200448 | tf_op jit(solution)/shard_map/while/body/eval_jaxpr/cos | solution.py:22
  592.2 8.0 %bitcast_add_fusion.2 = f32[512,1024]{0,1:T(8,128)} fusion(f32[512,1024]{0,1:T(8,128)S(1)} %copy.119, f32[1024,512]{1,0:T(8,128)S(1)} %copy-done.1, f32[1024,512]{1,0:T(8,128)S(1)} %get-tuple-element.673, f32[1024,512]{1,0:T(8,128)S(1)} %get-tuple-element.674), kind=kOutput, calls=%fused_computation.37.clone.1 | convolution fusion | flops 6444023808 | bytes 10485760 | tf_op jit(solution)/shard_map/while/body/eval_jaxpr/dot_general | solution.py:93
  (183 shorter events, 230.6 us)
Async XLA Ops:
  30.4 21.7 %all-to-all-start = ((f32[2,128,512]{2,0,1:T(2,128)}), f32[2,128,512]{2,0,1:T(2,128)S(1)}, u32[]{:S(2)}, u32[]{:S(2)}) async-start(f32[2,128,512]{2,0,1:T(2,128)} %copy.79), calls=%async_computation | async-start | bytes 1048576 | tf_op jit(solution)/shard_map/all_to_all | solution.py:114
  37.6 192.7 %all-reduce.2.cloned.1.call-start = ((), (), s32[]{:S(2)}) async-start(), calls=%async_computation.5 | async-start | bytes 1048576 | tf_op jit(solution)/shard_map/psum | solution.py:164
  53.6 54.0 %copy-start.6 = (f32[2,4,64,512]{3,2,1,0:T(8,128)S(1)}, f32[2,4,64,512]{3,2,1,0:T(8,128)}, u32[]{:S(2)}) copy-start(f32[2,4,64,512]{3,2,1,0:T(8,128)} %param.12) | copy-start | bytes 3145732
  101.2 6.6 %copy-start.2 = (f32[512,1024]{1,0:T(8,128)S(1)}, f32[512,1024]{1,0:T(8,128)}, u32[]{:S(2)}) copy-start(f32[512,1024]{1,0:T(8,128)} %get-tuple-element.581) | copy-start | bytes 6291460
  115.2 1.0 copy-start.5
  117.2 9.1 %collective-permute-start = (f32[64,2,4,128]{3,0,2,1:T(8,128)}, f32[64,2,4,128]{3,0,2,1:T(8,128)}, u32[]{:S(2)}, u32[]{:S(2)}) collective-permute-start(f32[64,2,4,128]{3,0,2,1:T(8,128)} %get-tuple-element.564), channel_id=1, source_target_pairs={{0,4},{4,0},{8,12},{12,8},{16,20},{20,16},{24,28},{28,24},{1,5},{5... | collective-permute-start | bytes 786440 | tf_op jit(solution)/shard_map/ppermute | solution.py:146
  118.7 18.1 %collective-permute-start.1 = (f32[64,2,4,128]{3,0,2,1:T(8,128)}, f32[64,2,4,128]{3,0,2,1:T(8,128)}, u32[]{:S(2)}, u32[]{:S(2)}) collective-permute-start(f32[64,2,4,128]{3,0,2,1:T(8,128)} %get-tuple-element.565), channel_id=1, source_target_pairs={{0,8},{4,12},{8,0},{12,4},{16,24},{20,28},{24,16},{28,20},{1,9},{5... | collective-permute-start | bytes 786440 | tf_op jit(solution)/shard_map/ppermute | solution.py:146
  118.7 35.0 %collective-permute-start.2 = (f32[64,2,4,128]{3,0,2,1:T(8,128)}, f32[64,2,4,128]{3,0,2,1:T(8,128)}, u32[]{:S(2)}, u32[]{:S(2)}) collective-permute-start(f32[64,2,4,128]{3,0,2,1:T(8,128)} %get-tuple-element.566), channel_id=1, source_target_pairs={{0,12},{4,8},{8,4},{12,0},{16,28},{20,24},{24,20},{28,16},{1,13},{... | collective-permute-start | bytes 786440 | tf_op jit(solution)/shard_map/ppermute | solution.py:146
  120.7 38.5 %collective-permute-start.3 = (f32[64,2,4,128]{3,0,2,1:T(8,128)}, f32[64,2,4,128]{3,0,2,1:T(8,128)}, u32[]{:S(2)}, u32[]{:S(2)}) collective-permute-start(f32[64,2,4,128]{3,0,2,1:T(8,128)} %get-tuple-element.567), channel_id=1, source_target_pairs={{0,16},{4,20},{8,24},{12,28},{16,0},{20,4},{24,8},{28,12},{1,17},{... | collective-permute-start | bytes 786440 | tf_op jit(solution)/shard_map/ppermute | solution.py:146
  122.7 41.1 %collective-permute-start.4 = (f32[64,2,4,128]{3,0,2,1:T(8,128)}, f32[64,2,4,128]{3,0,2,1:T(8,128)}, u32[]{:S(2)}, u32[]{:S(2)}) collective-permute-start(f32[64,2,4,128]{3,0,2,1:T(8,128)} %get-tuple-element.569), channel_id=1, source_target_pairs={{0,20},{4,16},{8,28},{12,24},{16,4},{20,0},{24,12},{28,8},{1,21},{... | collective-permute-start | bytes 786440 | tf_op jit(solution)/shard_map/ppermute | solution.py:146
  126.4 42.8 %collective-permute-start.5 = (f32[64,2,4,128]{3,0,2,1:T(8,128)}, f32[64,2,4,128]{3,0,2,1:T(8,128)S(1)}, u32[]{:S(2)}, u32[]{:S(2)}) collective-permute-start(f32[64,2,4,128]{3,0,2,1:T(8,128)} %get-tuple-element.568), channel_id=1, source_target_pairs={{0,24},{4,28},{8,16},{12,20},{16,8},{20,12},{24,0},{28,4},{1,25},{... | collective-permute-start | bytes 786440 | tf_op jit(solution)/shard_map/ppermute | solution.py:146
  136.8 35.5 %collective-permute-start.6 = (f32[64,2,4,128]{3,0,2,1:T(8,128)}, f32[64,2,4,128]{3,0,2,1:T(8,128)S(1)}, u32[]{:S(2)}, u32[]{:S(2)}) collective-permute-start(f32[64,2,4,128]{3,0,2,1:T(8,128)} %get-tuple-element.562), channel_id=1, source_target_pairs={{0,28},{4,24},{8,20},{12,16},{16,12},{20,8},{24,4},{28,0},{1,29},{... | collective-permute-start | bytes 786440 | tf_op jit(solution)/shard_map/ppermute | solution.py:146
  193.0 3.4 copy-start
  193.0 37.4 %copy-start.8 = (s32[128,1024]{1,0:T(8,128)S(1)}, s32[128,1024]{1,0:T(8,128)}, u32[]{:S(2)}) copy-start(s32[128,1024]{1,0:T(8,128)} %param.13) | copy-start | bytes 1572868
  197.2 160.9 %reduce-scatter.3.cloned.1.call-start = ((), (), s32[]{:S(2)}) async-start(), calls=%async_computation.6 | async-start | bytes 163840 | tf_op jit(solution)/shard_map/reduce_scatter | solution.py:195
  236.9 4.0 copy-start.3
  316.1 1.9 copy-start.4
  338.0 1.2 copy-start.7
  340.4 40.5 %reduce-scatter.5.cloned.1.call-start = ((), (), s32[]{:S(2)}) async-start(), calls=%async_computation.7 | async-start | bytes 163840 | tf_op jit(solution)/shard_map/reduce_scatter | solution.py:196
  341.1 158.0 %all-gather.2.cloned.1.call-start = ((), (), s32[]{:S(2)}) async-start(), calls=%async_computation.8 | async-start | bytes 2621440 | tf_op jit(solution)/shard_map/all_gather | solution.py:206
  509.1 8.3 %copy-start.1 = (f32[1024,512]{1,0:T(8,128)S(1)}, f32[1024,512]{1,0:T(8,128)}, u32[]{:S(2)}) copy-start(f32[1024,512]{1,0:T(8,128)} %get-tuple-element.770) | copy-start | bytes 6291460 | tf_op jit(solution)/shard_map/while
  534.0 8.3 %copy-start.1 = (f32[1024,512]{1,0:T(8,128)S(1)}, f32[1024,512]{1,0:T(8,128)}, u32[]{:S(2)}) copy-start(f32[1024,512]{1,0:T(8,128)} %get-tuple-element.770) | copy-start | bytes 6291460 | tf_op jit(solution)/shard_map/while
  558.9 8.3 %copy-start.1 = (f32[1024,512]{1,0:T(8,128)S(1)}, f32[1024,512]{1,0:T(8,128)}, u32[]{:S(2)}) copy-start(f32[1024,512]{1,0:T(8,128)} %get-tuple-element.770) | copy-start | bytes 6291460 | tf_op jit(solution)/shard_map/while
  583.9 8.3 %copy-start.1 = (f32[1024,512]{1,0:T(8,128)S(1)}, f32[1024,512]{1,0:T(8,128)}, u32[]{:S(2)}) copy-start(f32[1024,512]{1,0:T(8,128)} %get-tuple-element.770) | copy-start | bytes 6291460 | tf_op jit(solution)/shard_map/while
Sparse Core Ops, SparseCore 0:
  197.4 32.9 all-reduce.1
  340.5 17.5 reduce-scatter.2
  361.3 19.5 reduce-scatter.4
  478.4 20.7 all-gather.1
